TPU v7x, 256 devices: a whole 4x4x8 slice. The times are simulated.
256 devices in a mesh: attn: 64 (over x, z, core), tp: 4 (over y).
Axes of the slice: x: 4, y: 4, z: 8, core: 2. Of those that a mesh axis runs over, the one named last changes fastest.
Arguments:
- lengths: int32 [32], replicated, may hold values from 1 to 4, 64 in all
- queries: bfloat16 [32768, 2560], P('attn', 'tp'), may hold values from -8 to 8
- key_vectors: bfloat16 [32768, 512], P('attn', 'tp'), may hold values from -8 to 8
- value_vectors: bfloat16 [32768, 512], P('attn', 'tp'), may hold values from -6 to 6
- out_weight: bfloat16 [2560, 5120], P('tp'), may hold values from -0.125 to 0.125
- grad_output: bfloat16 [32768, 5120], P(('attn', 'tp')), may hold values from -6 to 6
Outputs:
- layer_out: bfloat16 [32768, 5120], P(('attn', 'tp'))
- grad_queries: bfloat16 [32768, 2560], P('attn', 'tp')
- grad_keys: bfloat16 [32768, 512], P('attn', 'tp')
- grad_values: bfloat16 [32768, 512], P('attn', 'tp')
Inputs may be any that keep to these rules, and one draw needn't show every extreme that they name: Document d covers lengths[d] whole blocks of 512 tokens; the documents follow one another and fill all 64 blocks; the longest covers exactly 4 blocks.
All inputs are finite; a program needn't handle non-finite values.
Results may differ from a plain program's by a relative error of at most 0.019.
Values may be sent and summed in bfloat16 or wider, within the bound.
A program may use at most 64 MiB of HBM per device.

v0:
```python
import jax
import jax.numpy as jnp
from jax import lax
from jax.sharding import PartitionSpec as P

HEAD_DIM = 128
MOST_CH = 4
GROUP = 5


NEGATIVE = -1e30


def from_behind(x, axis, by):
    devices = lax.axis_size(axis)
    pairs = [(i, i + by) for i in range(devices) if 0 <= i + by < devices]
    return lax.ppermute(x, axis, pairs)


def masked_scores(query_blk, key_blk, offset):
    tok = query_blk.shape[0]
    logits = jnp.einsum(
        "tgrd,ugd->grtu", query_blk, key_blk, preferred_element_type=jnp.float32
    ) * HEAD_DIM ** (-0.5)
    rows_at = lax.broadcasted_iota(jnp.int32, (tok, tok), 0)
    cols_at = lax.broadcasted_iota(jnp.int32, (tok, tok), 1)
    keep = (offset > 0) | (cols_at <= rows_at)
    return jnp.where(keep, logits, NEGATIVE)


def span_stats(query_blk, fetch, depth, reach):
    stat_shape = (query_blk.shape[1], query_blk.shape[2], query_blk.shape[0])

    def step(offset, carry):

        def live(carry):
            top, total = carry
            key_blk, value_blk = fetch(offset)
            logits = masked_scores(query_blk, key_blk, offset)
            new_top = jnp.maximum(top, jnp.max(logits, axis=-1))
            total = total * jnp.exp(top - new_top) + jnp.sum(
                jnp.exp(logits - new_top[..., None]), axis=-1
            )
            return (new_top, total)

        def skipped(carry):
            return carry

        return lax.cond(offset <= depth, live, skipped, carry)

    start = (jnp.full(stat_shape, NEGATIVE, jnp.float32), jnp.zeros(stat_shape, jnp.float32))
    top, total = lax.fori_loop(0, reach, step, start)
    return top + jnp.log(total)


def span_output(query_blk, fetch, depth, reach, log_total):

    def step(offset, accum):

        def live(accum):
            key_blk, value_blk = fetch(offset)
            logits = masked_scores(query_blk, key_blk, offset)
            weights = jnp.exp(logits - log_total[..., None]).astype(jnp.bfloat16)
            return accum + jnp.einsum(
                "grtu,ugd->tgrd", weights, value_blk, preferred_element_type=jnp.float32
            )

        def skipped(accum):
            return accum

        return lax.cond(offset <= depth, live, skipped, accum)

    accum = lax.fori_loop(0, reach, step, jnp.zeros(query_blk.shape, jnp.float32))
    return accum.astype(jnp.bfloat16)


def task_grads(query_blk, grad_blk, log_total, delta, key_blk, value_blk, offset):
    logits = masked_scores(query_blk, key_blk, offset)
    probs = jnp.exp(logits - log_total[..., None])
    probs_low = probs.astype(jnp.bfloat16)
    dprobs = jnp.einsum("tgrd,ugd->grtu", grad_blk, value_blk, preferred_element_type=jnp.float32)
    dlogits = (probs * (dprobs - delta[..., None])).astype(jnp.bfloat16)
    grad_q = jnp.einsum("grtu,ugd->tgrd", dlogits, key_blk, preferred_element_type=jnp.float32)
    grad_k = jnp.einsum(
        "grtu,tgrd->ugd", dlogits, query_blk, preferred_element_type=jnp.float32
    ) * HEAD_DIM ** (-0.5)
    grad_v = jnp.einsum("grtu,tgrd->ugd", probs_low, grad_blk, preferred_element_type=jnp.float32)
    return (grad_q, grad_k, grad_v)


def on_device(lengths, queries, key_vectors, value_vectors, out_weight, grad_output):
    tok = queries.shape[0]
    local_kv = key_vectors.shape[1] // HEAD_DIM
    half_width = local_kv * HEAD_DIM
    reach = MOST_CH
    block = lax.axis_index("attn")
    ends = jnp.cumsum(lengths)
    owner = jnp.sum((block >= ends).astype(jnp.int32))
    starts = ends - lengths
    first = jnp.sum(jnp.where(jnp.arange(lengths.shape[0], dtype=jnp.int32) == owner, starts, 0))
    depth = block - first
    query_blk = queries.reshape(tok, local_kv, GROUP, HEAD_DIM)
    paired = jnp.concatenate([key_vectors, value_vectors], axis=1)

    def grab(offset, carry):
        current, stored = carry
        current = from_behind(current, "attn", 1)
        return (current, lax.dynamic_update_index_in_dim(stored, current, offset, 0))

    stored = jnp.zeros((reach, tok, 2 * half_width), jnp.bfloat16).at[0].set(paired)
    current, stored = lax.fori_loop(1, reach, grab, (paired, stored))

    def fetch(offset):
        piece = lax.dynamic_index_in_dim(stored, offset, 0, keepdims=False)
        return (
            piece[:, :half_width].reshape(tok, local_kv, HEAD_DIM),
            piece[:, half_width:].reshape(tok, local_kv, HEAD_DIM),
        )

    log_total = span_stats(query_blk, fetch, depth, reach)
    out_blk = span_output(query_blk, fetch, depth, reach, log_total)
    attn_out = out_blk.reshape(tok, local_kv * GROUP * HEAD_DIM)
    layer_out = lax.psum_scatter(
        jnp.dot(attn_out, out_weight, preferred_element_type=jnp.float32).astype(jnp.bfloat16),
        "tp",
        scatter_dimension=0,
        tiled=True,
    )
    grad_attn = lax.dot_general(
        lax.all_gather(grad_output, "tp", axis=0, tiled=True),
        out_weight,
        (((1,), (1,)), ((), ())),
        preferred_element_type=jnp.float32,
    ).astype(jnp.bfloat16)
    grad_blk = grad_attn.reshape(tok, local_kv, GROUP, HEAD_DIM)
    delta = jnp.transpose(
        jnp.sum(grad_blk.astype(jnp.float32) * out_blk.astype(jnp.float32), axis=-1), (1, 2, 0)
    )

    def task(offset, grad_q):

        def live(grad_q):
            key_blk, value_blk = fetch(offset)
            part_q, part_k, part_v = task_grads(
                query_blk, grad_blk, log_total, delta, key_blk, value_blk, offset
            )
            joined = jnp.concatenate(
                [part_k.reshape(tok, half_width), part_v.reshape(tok, half_width)], axis=1
            )
            return (grad_q + part_q, joined)

        def skipped(grad_q):
            return (grad_q, jnp.zeros((tok, 2 * half_width), jnp.float32))

        return lax.cond(offset <= depth, live, skipped, grad_q)

    zero_q = jnp.zeros(query_blk.shape, jnp.float32)

    def back_step(index, carry):
        grad_q, travel = carry
        offset = reach - 1 - index
        grad_q, joined = task(offset, grad_q)
        travel = from_behind((travel + joined).astype(jnp.bfloat16), "attn", -1).astype(jnp.float32)
        return (grad_q, travel)

    grad_q, travel = lax.fori_loop(
        0, reach - 1, back_step, (zero_q, jnp.zeros((tok, 2 * half_width), jnp.float32))
    )
    grad_q, joined = task(0, grad_q)
    grad_pairs = travel + joined
    grad_queries = (
        (grad_q * HEAD_DIM ** (-0.5)).astype(jnp.bfloat16).reshape(tok, local_kv * GROUP * HEAD_DIM)
    )
    grad_keys = grad_pairs[:, :half_width].astype(jnp.bfloat16)
    grad_values = grad_pairs[:, half_width:].astype(jnp.bfloat16)
    return (layer_out, grad_queries, grad_keys, grad_values)


def solution(mesh):
    return jax.shard_map(
        on_device,
        mesh=mesh,
        in_specs=(
            P(),
            P("attn", "tp"),
            P("attn", "tp"),
            P("attn", "tp"),
            P("tp", None),
            P(("attn", "tp"), None),
        ),
        out_specs=(P(("attn", "tp"), None), P("attn", "tp"), P("attn", "tp"), P("attn", "tp")),
        check_vma=False,
    )
```

profile of v0, /device:TPU:135, one launch (start us, length us, event | category | flops | bytes accessed | tf_op | source)
XLA Modules:
  0.0 184.4 jit_solution(55842613366538888)
XLA Ops:
  9.5 1.9 %fusion.71 = s32[]{:T(128)} fusion(s32[32]{0:T(128)S(1)} %reduce.5, s32[32]{0:T(128)} %param.24, s32[]{:T(128)} %fusion.70), kind=kLoop, calls=%fused_computation.100 | loop fusion | flops 127 | bytes 264 | tf_op jit(solution)/shard_map/reduce_sum | solution.py:100
  12.1 1.3 copy.49
  15.7 22.1 %while.69 = (s32[]{:T(128)}, bf16[512,256]{1,0:T(8,128)(2,1)S(1)}, bf16[4,512,256]{2,1,0:T(8,128)(2,1)S(1)}, s32[]{:T(128)}, s32[]{:T(128)}, /*index=5*/s32[]{:T(128)}) while((s32[]{:T(128)}, bf16[512,256]{1,0:T(8,128)(2,1)S(1)}, bf16[4,512,256]{2,1,0:T(8,128)(2,1)S(1)}, s32[]{:T(128)}, s32[]{:T(128)}, /*index=5*/s32[]{:T(128)}) %tuple.174), condition=%wide.region_4.5_spmd, body=%wide.region_3.4_spmd.sunk | while | flops 5 | bytes 2097307 | solution.py:111
  15.7 3.2 %collective-permute-start = (bf16[512,256]{1,0:T(8,128)(2,1)S(1)}, bf16[512,256]{1,0:T(8,128)(2,1)S(1)}, u32[]{:S(2)}, u32[]{:S(2)}) collective-permute-start(bf16[512,256]{1,0:T(8,128)(2,1)S(1)} %get-tuple-element.865), channel_id=1, source_target_pairs={{0,4},{4,8},{8,12},{12,16},{16,20},{20,24},{24,28},{28,32},{32,36}... | collective-permute-start | bytes 786440 | tf_op jit(solution)/shard_map/while/body/eval_jaxpr/ppermute | solution.py:17
  18.9 3.3 %collective-permute-done = bf16[512,256]{1,0:T(8,128)(2,1)S(1)} collective-permute-done((bf16[512,256]{1,0:T(8,128)(2,1)S(1)}, bf16[512,256]{1,0:T(8,128)(2,1)S(1)}, u32[]{:S(2)}, u32[]{:S(2)}) %collective-permute-start) | collective-permute-done | bytes 262176 | tf_op jit(solution)/shard_map/while/body/eval_jaxpr/ppermute | solution.py:17
  22.3 4.4 %collective-permute-start = (bf16[512,256]{1,0:T(8,128)(2,1)S(1)}, bf16[512,256]{1,0:T(8,128)(2,1)S(1)}, u32[]{:S(2)}, u32[]{:S(2)}) collective-permute-start(bf16[512,256]{1,0:T(8,128)(2,1)S(1)} %get-tuple-element.865), channel_id=1, source_target_pairs={{0,4},{4,8},{8,12},{12,16},{16,20},{20,24},{24,28},{28,32},{32,36}... | collective-permute-start | bytes 786440 | tf_op jit(solution)/shard_map/while/body/eval_jaxpr/ppermute | solution.py:17
  26.7 3.3 %collective-permute-done = bf16[512,256]{1,0:T(8,128)(2,1)S(1)} collective-permute-done((bf16[512,256]{1,0:T(8,128)(2,1)S(1)}, bf16[512,256]{1,0:T(8,128)(2,1)S(1)}, u32[]{:S(2)}, u32[]{:S(2)}) %collective-permute-start) | collective-permute-done | bytes 262176 | tf_op jit(solution)/shard_map/while/body/eval_jaxpr/ppermute | solution.py:17
  30.0 4.4 %collective-permute-start = (bf16[512,256]{1,0:T(8,128)(2,1)S(1)}, bf16[512,256]{1,0:T(8,128)(2,1)S(1)}, u32[]{:S(2)}, u32[]{:S(2)}) collective-permute-start(bf16[512,256]{1,0:T(8,128)(2,1)S(1)} %get-tuple-element.865), channel_id=1, source_target_pairs={{0,4},{4,8},{8,12},{12,16},{16,20},{20,24},{24,28},{28,32},{32,36}... | collective-permute-start | bytes 786440 | tf_op jit(solution)/shard_map/while/body/eval_jaxpr/ppermute | solution.py:17
  34.5 3.3 %collective-permute-done = bf16[512,256]{1,0:T(8,128)(2,1)S(1)} collective-permute-done((bf16[512,256]{1,0:T(8,128)(2,1)S(1)}, bf16[512,256]{1,0:T(8,128)(2,1)S(1)}, u32[]{:S(2)}, u32[]{:S(2)}) %collective-permute-start) | collective-permute-done | bytes 262176 | tf_op jit(solution)/shard_map/while/body/eval_jaxpr/ppermute | solution.py:17
  37.8 7.2 %while.70 = (s32[]{:T(128)}, f32[1,5,512]{2,1,0:T(8,128)S(1)}, f32[1,5,512]{2,1,0:T(8,128)S(1)}, s32[]{:T(128)}, bf16[4,512,256]{2,1,0:T(8,128)(2,1)S(1)}, /*index=5*/bf16[512,1,5,128]{3,0,2,1:T(8,128)(2,1)S(1)}, s32[]{:T(128)}) while((s32[]{:T(128)}, f32[1,5,512]{2,1,0:T(8,128)S(1)}, f32[1,5,512]{2,1,0:T(8,128)S(1)}, s32[]{:T(128)}, ...), condition=%wide.region_10.11_spmd, body=%wide.region_5.0_spmd.sunk | while | flops 345248768 | bytes 12716251 | solution.py:52
  37.8 2.4 %conditional.9 = ((f32[1,5,512]{2,1,0:T(8,128)S(1)}, f32[1,5,512]{2,1,0:T(8,128)S(1)})) conditional(s32[]{:T(128)} %convert_element_type.136, (f32[1,5,512]{2,1,0:T(8,128)S(1)}, f32[1,5,512]{2,1,0:T(8,128)S(1)}) %tuple.164, (s32[]{:T(128)}, bf16[4,512,256]{2,1,0:T(8,128)(2,1)S(1)}, bf16[512,1,5,128]{3,0,2,1:T(8,128)(2,1)S(1)}, ...), branch_computations={%region_6.6_spmd, %region_7.9_spmd} | conditional | flops 345248768 | bytes 12716104 | solution.py:49
  40.2 2.3 %conditional.9 = ((f32[1,5,512]{2,1,0:T(8,128)S(1)}, f32[1,5,512]{2,1,0:T(8,128)S(1)})) conditional(s32[]{:T(128)} %convert_element_type.136, (f32[1,5,512]{2,1,0:T(8,128)S(1)}, f32[1,5,512]{2,1,0:T(8,128)S(1)}) %tuple.164, (s32[]{:T(128)}, bf16[4,512,256]{2,1,0:T(8,128)(2,1)S(1)}, bf16[512,1,5,128]{3,0,2,1:T(8,128)(2,1)S(1)}, ...), branch_computations={%region_6.6_spmd, %region_7.9_spmd} | conditional | flops 345248768 | bytes 12716104 | solution.py:49
  42.6 2.4 %conditional.9 = ((f32[1,5,512]{2,1,0:T(8,128)S(1)}, f32[1,5,512]{2,1,0:T(8,128)S(1)})) conditional(s32[]{:T(128)} %convert_element_type.136, (f32[1,5,512]{2,1,0:T(8,128)S(1)}, f32[1,5,512]{2,1,0:T(8,128)S(1)}) %tuple.164, (s32[]{:T(128)}, bf16[4,512,256]{2,1,0:T(8,128)(2,1)S(1)}, bf16[512,1,5,128]{3,0,2,1:T(8,128)(2,1)S(1)}, ...), branch_computations={%region_6.6_spmd, %region_7.9_spmd} | conditional | flops 345248768 | bytes 12716104 | solution.py:49
  46.8 13.3 %while.71 = (s32[]{:T(128)}, f32[512,1,5,128]{0,3,2,1:T(8,128)}, s32[]{:T(128)}, bf16[4,512,256]{2,1,0:T(8,128)(2,1)S(1)}, bf16[512,1,5,128]{3,0,2,1:T(8,128)(2,1)S(1)}, /*index=5*/f32[1,5,512]{2,1,0:T(8,128)}, s32[]{:T(128)}) while((s32[]{:T(128)}, f32[512,1,5,128]{0,3,2,1:T(8,128)}, s32[]{:T(128)}, bf16[4,512,256]{2,1,0:T(8,128)(2,1)S(1)}, ...), condition=%wide.region_14.15_spmd, body=%wide.region_11.14_spmd.sunk | while | flops 677183488 | bytes 4597947 | solution.py:73
  46.8 4.5 %conditional.10 = (f32[512,1,5,128]{0,3,2,1:T(8,128)}) conditional(s32[]{:T(128)} %convert_element_type.137, f32[512,1,5,128]{0,3,2,1:T(8,128)} %get-tuple-element.905, (s32[]{:T(128)}, bf16[4,512,256]{2,1,0:T(8,128)(2,1)S(1)}, bf16[512,1,5,128]{3,0,2,1:T(8,128)(2,1)S(1)}, f32[1,5,512]{2,1,0:T(8,128)}, f32[512,1,5,128]{0,3,2,1:T(8,128)}) %tuple.167), branch_computations={%region_12.12_spmd, %region_13.13_spmd} | conditional | flops 677183488 | bytes 4597816 | solution.py:71
  47.0 4.3 %fusion.16 = f32[512,1,5,128]{0,3,2,1:T(8,128)} fusion(f32[512,1,5,128]{0,3,2,1:T(8,128)} %get-tuple-element.500, f32[5,512]{1,0:T(8,128)} %bitcast.15, pred[512,512]{0,1:T(8,128)(4,1)S(1)} %fusion.19, bf16[512,1,5,128]{3,0,2,1:T(8,128)(2,1)S(1)} %get-tuple-element.503, bf16[512,256]{1,0:T(8,128)(2,1)S(1)} %dynamic-slice_bitcast_fusion.1), kind=kOutput, calls=%fused_computation.21 | convolution fusion | flops 676659200 | bytes 3811328 | tf_op jit(solution)/shard_map/while/body/eval_jaxpr/cond/branch_1_fun/grtu,ugd->tgrd/dot_general | solution.py:64
  51.3 4.4 %conditional.10 = (f32[512,1,5,128]{0,3,2,1:T(8,128)}) conditional(s32[]{:T(128)} %convert_element_type.137, f32[512,1,5,128]{0,3,2,1:T(8,128)} %get-tuple-element.905, (s32[]{:T(128)}, bf16[4,512,256]{2,1,0:T(8,128)(2,1)S(1)}, bf16[512,1,5,128]{3,0,2,1:T(8,128)(2,1)S(1)}, f32[1,5,512]{2,1,0:T(8,128)}, f32[512,1,5,128]{0,3,2,1:T(8,128)}) %tuple.167), branch_computations={%region_12.12_spmd, %region_13.13_spmd} | conditional | flops 677183488 | bytes 4597816 | solution.py:71
  51.4 4.3 %fusion.16 = f32[512,1,5,128]{0,3,2,1:T(8,128)} fusion(f32[512,1,5,128]{0,3,2,1:T(8,128)} %get-tuple-element.500, f32[5,512]{1,0:T(8,128)} %bitcast.15, pred[512,512]{0,1:T(8,128)(4,1)S(1)} %fusion.19, bf16[512,1,5,128]{3,0,2,1:T(8,128)(2,1)S(1)} %get-tuple-element.503, bf16[512,256]{1,0:T(8,128)(2,1)S(1)} %dynamic-slice_bitcast_fusion.1), kind=kOutput, calls=%fused_computation.21 | convolution fusion | flops 676659200 | bytes 3811328 | tf_op jit(solution)/shard_map/while/body/eval_jaxpr/cond/branch_1_fun/grtu,ugd->tgrd/dot_general | solution.py:64
  55.7 4.4 %conditional.10 = (f32[512,1,5,128]{0,3,2,1:T(8,128)}) conditional(s32[]{:T(128)} %convert_element_type.137, f32[512,1,5,128]{0,3,2,1:T(8,128)} %get-tuple-element.905, (s32[]{:T(128)}, bf16[4,512,256]{2,1,0:T(8,128)(2,1)S(1)}, bf16[512,1,5,128]{3,0,2,1:T(8,128)(2,1)S(1)}, f32[1,5,512]{2,1,0:T(8,128)}, f32[512,1,5,128]{0,3,2,1:T(8,128)}) %tuple.167), branch_computations={%region_12.12_spmd, %region_13.13_spmd} | conditional | flops 677183488 | bytes 4597816 | solution.py:71
  55.9 4.3 %fusion.16 = f32[512,1,5,128]{0,3,2,1:T(8,128)} fusion(f32[512,1,5,128]{0,3,2,1:T(8,128)} %get-tuple-element.500, f32[5,512]{1,0:T(8,128)} %bitcast.15, pred[512,512]{0,1:T(8,128)(4,1)S(1)} %fusion.19, bf16[512,1,5,128]{3,0,2,1:T(8,128)(2,1)S(1)} %get-tuple-element.503, bf16[512,256]{1,0:T(8,128)(2,1)S(1)} %dynamic-slice_bitcast_fusion.1), kind=kOutput, calls=%fused_computation.21 | convolution fusion | flops 676659200 | bytes 3811328 | tf_op jit(solution)/shard_map/while/body/eval_jaxpr/cond/branch_1_fun/grtu,ugd->tgrd/dot_general | solution.py:64
  60.2 10.7 %all-gather.2.cloned.1.call-done = bf16[512,5120]{1,0:T(8,128)(2,1)} async-done(((bf16[128,5120]{1,0:T(8,128)(2,1)}), bf16[512,5120]{1,0:T(8,128)(2,1)}) %all-gather.2.cloned.1.call-update) | async-done | bytes 5242896 | tf_op jit(solution)/shard_map/all_gather | solution.py:130
  70.9 9.5 %convolution_convert_fusion.1 = bf16[512,640]{1,0:T(8,128)(2,1)} fusion(bf16[512,5120]{1,0:T(8,128)(2,1)} %all-gather.2.cloned.1.call-done, bf16[640,5120]{1,0:T(8,128)(2,1)} %param.28), kind=kOutput, calls=%fused_computation.90 | convolution fusion | flops 3355770880 | bytes 12451840 | tf_op jit(solution)/shard_map/dot_general | solution.py:129
  80.4 2.2 %copy.52 = bf16[512,640]{0,1:T(8,128)(2,1)} copy(bf16[512,640]{1,0:T(8,128)(2,1)} %convolution_convert_fusion.1) | data formatting | bytes 1310720 | tf_op jit(solution)/shard_map/convert_element_type | solution.py:134
  82.5 1.3 multiply_reduce_fusion
  83.9 8.9 %convolution_convert_fusion = bf16[512,5120]{1,0:T(8,128)(2,1)} fusion(bf16[512,640]{0,1:T(8,128)(2,1)S(1)} %bitcast.239, bf16[640,5120]{1,0:T(8,128)(2,1)} %param.28), kind=kOutput, calls=%fused_computation.89 | convolution fusion | flops 3358064640 | bytes 12451840 | tf_op jit(solution)/shard_map/dot_general | solution.py:124
  93.0 67.0 %while.72 = (s32[]{:T(128)}, f32[512,1,5,128]{0,3,2,1:T(8,128)S(1)}, f32[512,256]{0,1:T(8,128)}, s32[]{:T(128)}, bf16[4,512,256]{2,1,0:T(8,128)(2,1)S(1)}, /*ind...) while((s32[]{:T(128)}, ...), condition=%wide.region_20.21_spmd.clone, body=%wide.region_17.20_spmd.clone.sunk | while | flops 1692401664 | bytes 55742904 | solution.py:166
  94.1 2.6 %collective-permute-start.1 = (bf16[512,256]{0,1:T(8,128)(2,1)}, bf16[512,256]{0,1:T(8,128)(2,1)S(1)}, u32[]{:S(2)}, u32[]{:S(2)}) collective-permute-start(bf16[512,256]{0,1:T(8,128)(2,1)} %fusion.82), channel_id=1, source_target_pairs={{4,0},{8,4},{12,8},{16,12},{20,16},{24,20},{28,24},{32,28},{36,32}... | collective-permute-start | bytes 786440 | tf_op jit(solution)/shard_map/while/body/eval_jaxpr/ppermute | solution.py:17
  96.7 16.8 %collective-permute-done.1 = bf16[512,256]{0,1:T(8,128)(2,1)S(1)} collective-permute-done((bf16[512,256]{0,1:T(8,128)(2,1)}, bf16[512,256]{0,1:T(8,128)(2,1)S(1)}, u32[]{:S(2)}, u32[]{:S(2)}) %collective-permute-start.1) | collective-permute-done | bytes 262176 | tf_op jit(solution)/shard_map/while/body/eval_jaxpr/ppermute | solution.py:17
  114.3 12.0 %conditional.11 = (f32[512,1,5,128]{0,3,2,1:T(8,128)S(1)}, f32[512,256]{0,1:T(8,128)S(1)}) conditional(s32[]{:T(128)} %convert_element_type.139, f32[512,1,5,128]{0,3,2,1:T(8,128)S(1)} %get-tuple-element.931, (s32[]{:T(128)}, bf16[4,512,256]{2,1,0:T(8,128)(2,1)S(1)}, bf16[512,1,5,128]{0,3,2,1:T(8,128)(2,1)S(1)}, f32[1,5,512]{2,1,0:T(8,128)}, ...), branch_computations={%region_18.18_spmd, %region_19.19_spmd} | conditional | flops 1691877376 | bytes 52596932 | solution.py:155
  114.4 3.2 %fusion.43 = f32[512,512,5]{1,0,2:T(8,128)} fusion(bf16[512,1,5,128]{0,3,2,1:T(8,128)(2,1)S(1)} %get-tuple-element.515, bf16[512,256]{1,0:T(8,128)(2,1)S(1)} %dynamic-slice_bitcast_fusion.2), kind=kOutput, calls=%fused_computation.51 | convolution fusion | flops 335544320 | bytes 6029312 | tf_op jit(solution)/shard_map/while/body/eval_jaxpr/cond/branch_1_fun/tgrd,ugd->grtu/dot_general | solution.py:22
  117.7 4.6 %fusion.30 = bf16[5,512,512]{1,2,0:T(8,128)(2,1)S(1)} fusion(f32[512,512,5]{1,0,2:T(8,128)} %fusion.43, f32[5,512]{1,0:T(8,128)S(1)} %bitcast.242, f32[5,512]{1,0:T(8,128)} %bitcast.25, pred[512,512]{0,1:T(8,128)(4,1)S(1)} %fusion.39, bf16[512,1,5,128]{0,3,2,1:T(8,128)(2,1)} %get-tuple-element.517, bf16[512,256]{1,0:T(8,128)(2,1)S(1)} %dynamic-slice_bitcast_fusion.2), kind=kOutput, calls=%fused_computation.38 | convolution fusion | flops 343408640 | bytes 8939520 | tf_op jit(solution)/shard_map/while/body/eval_jaxpr/cond/branch_1_fun/tgrd,ugd->grtu/dot_general | solution.py:81
  123.3 2.4 %fusion.36 = f32[512,128]{0,1:T(8,128)S(1)} fusion(f32[512,512,5]{1,0,2:T(8,128)S(1)} %bitcast.232, f32[5,512]{1,0:T(8,128)} %bitcast.25, pred[512,512]{0,1:T(8,128)(4,1)S(1)} %fusion.39, bf16[512,1,5,128]{0,3,2,1:T(8,128)(2,1)S(1)} %copy-done.4), kind=kOutput, calls=%fused_computation.45 | convolution fusion | flops 340787200 | bytes 6432768 | tf_op jit(solution)/shard_map/while/body/eval_jaxpr/cond/branch_1_fun/grtu,tgrd->ugd/dot_general | solution.py:87
  126.4 1.9 %fusion.82 = bf16[512,256]{0,1:T(8,128)(2,1)} fusion(f32[512,256]{0,1:T(8,128)S(1)} %get-tuple-element.849, f32[512,256]{0,1:T(8,128)} %get-tuple-element.932, pred[]{:T(512)S(6)} %compare.10), kind=kLoop, calls=%fused_computation.88.clone.1 | loop fusion | flops 393216 | bytes 1310721 | tf_op jit(solution)/shard_map/while/body/eval_jaxpr/convert_element_type | solution.py:163
  128.3 1.9 %collective-permute-start.1 = (bf16[512,256]{0,1:T(8,128)(2,1)}, bf16[512,256]{0,1:T(8,128)(2,1)S(1)}, u32[]{:S(2)}, u32[]{:S(2)}) collective-permute-start(bf16[512,256]{0,1:T(8,128)(2,1)} %fusion.82), channel_id=1, source_target_pairs={{4,0},{8,4},{12,8},{16,12},{20,16},{24,20},{28,24},{32,28},{36,32}... | collective-permute-start | bytes 786440 | tf_op jit(solution)/shard_map/while/body/eval_jaxpr/ppermute | solution.py:17
  130.2 6.4 %collective-permute-done.1 = bf16[512,256]{0,1:T(8,128)(2,1)S(1)} collective-permute-done((bf16[512,256]{0,1:T(8,128)(2,1)}, bf16[512,256]{0,1:T(8,128)(2,1)S(1)}, u32[]{:S(2)}, u32[]{:S(2)}) %collective-permute-start.1) | collective-permute-done | bytes 262176 | tf_op jit(solution)/shard_map/while/body/eval_jaxpr/ppermute | solution.py:17
  137.4 12.0 %conditional.11 = (f32[512,1,5,128]{0,3,2,1:T(8,128)S(1)}, f32[512,256]{0,1:T(8,128)S(1)}) conditional(s32[]{:T(128)} %convert_element_type.139, f32[512,1,5,128]{0,3,2,1:T(8,128)S(1)} %get-tuple-element.931, (s32[]{:T(128)}, bf16[4,512,256]{2,1,0:T(8,128)(2,1)S(1)}, bf16[512,1,5,128]{0,3,2,1:T(8,128)(2,1)S(1)}, f32[1,5,512]{2,1,0:T(8,128)}, ...), branch_computations={%region_18.18_spmd, %region_19.19_spmd} | conditional | flops 1691877376 | bytes 52596932 | solution.py:155
  137.5 3.2 %fusion.43 = f32[512,512,5]{1,0,2:T(8,128)} fusion(bf16[512,1,5,128]{0,3,2,1:T(8,128)(2,1)S(1)} %get-tuple-element.515, bf16[512,256]{1,0:T(8,128)(2,1)S(1)} %dynamic-slice_bitcast_fusion.2), kind=kOutput, calls=%fused_computation.51 | convolution fusion | flops 335544320 | bytes 6029312 | tf_op jit(solution)/shard_map/while/body/eval_jaxpr/cond/branch_1_fun/tgrd,ugd->grtu/dot_general | solution.py:22
  140.7 4.6 %fusion.30 = bf16[5,512,512]{1,2,0:T(8,128)(2,1)S(1)} fusion(f32[512,512,5]{1,0,2:T(8,128)} %fusion.43, f32[5,512]{1,0:T(8,128)S(1)} %bitcast.242, f32[5,512]{1,0:T(8,128)} %bitcast.25, pred[512,512]{0,1:T(8,128)(4,1)S(1)} %fusion.39, bf16[512,1,5,128]{0,3,2,1:T(8,128)(2,1)} %get-tuple-element.517, bf16[512,256]{1,0:T(8,128)(2,1)S(1)} %dynamic-slice_bitcast_fusion.2), kind=kOutput, calls=%fused_computation.38 | convolution fusion | flops 343408640 | bytes 8939520 | tf_op jit(solution)/shard_map/while/body/eval_jaxpr/cond/branch_1_fun/tgrd,ugd->grtu/dot_general | solution.py:81
  146.3 2.4 %fusion.36 = f32[512,128]{0,1:T(8,128)S(1)} fusion(f32[512,512,5]{1,0,2:T(8,128)S(1)} %bitcast.232, f32[5,512]{1,0:T(8,128)} %bitcast.25, pred[512,512]{0,1:T(8,128)(4,1)S(1)} %fusion.39, bf16[512,1,5,128]{0,3,2,1:T(8,128)(2,1)S(1)} %copy-done.4), kind=kOutput, calls=%fused_computation.45 | convolution fusion | flops 340787200 | bytes 6432768 | tf_op jit(solution)/shard_map/while/body/eval_jaxpr/cond/branch_1_fun/grtu,tgrd->ugd/dot_general | solution.py:87
  149.4 1.9 %fusion.82 = bf16[512,256]{0,1:T(8,128)(2,1)} fusion(f32[512,256]{0,1:T(8,128)S(1)} %get-tuple-element.849, f32[512,256]{0,1:T(8,128)} %get-tuple-element.932, pred[]{:T(512)S(6)} %compare.10), kind=kLoop, calls=%fused_computation.88.clone.1 | loop fusion | flops 393216 | bytes 1310721 | tf_op jit(solution)/shard_map/while/body/eval_jaxpr/convert_element_type | solution.py:163
  151.3 1.9 %collective-permute-start.1 = (bf16[512,256]{0,1:T(8,128)(2,1)}, bf16[512,256]{0,1:T(8,128)(2,1)S(1)}, u32[]{:S(2)}, u32[]{:S(2)}) collective-permute-start(bf16[512,256]{0,1:T(8,128)(2,1)} %fusion.82), channel_id=1, source_target_pairs={{4,0},{8,4},{12,8},{16,12},{20,16},{24,20},{28,24},{32,28},{36,32}... | collective-permute-start | bytes 786440 | tf_op jit(solution)/shard_map/while/body/eval_jaxpr/ppermute | solution.py:17
  153.2 6.0 %collective-permute-done.1 = bf16[512,256]{0,1:T(8,128)(2,1)S(1)} collective-permute-done((bf16[512,256]{0,1:T(8,128)(2,1)}, bf16[512,256]{0,1:T(8,128)(2,1)S(1)}, u32[]{:S(2)}, u32[]{:S(2)}) %collective-permute-start.1) | collective-permute-done | bytes 262176 | tf_op jit(solution)/shard_map/while/body/eval_jaxpr/ppermute | solution.py:17
  160.0 1.2 copy.56
  161.2 12.8 %conditional.4 = (f32[512,1,5,128]{3,0,2,1:T(8,128)S(1)}, f32[512,256]{1,0:T(8,128)}) conditional(s32[]{:T(128)} %convert_element_type.87, (f32[512,1,5,128]{0,3,2,1:T(8,128)S(1)}) %tuple.126, (bf16[4,512,256]{2,1,0:T(8,128)(2,1)S(1)}, bf16[512,1,5,128]{0,3,2,1:T(8,128)(2,1)S(1)}, f32[1,5,512]{2,1,0:T(8,128)}, bf16[512,1,5,128]{0,3,2,1:T(8,128)(2,1)}, ...), branch_computations={%region_21.22_spmd, %region_22.23_spmd} | conditional | flops 1691615232 | bytes 51024000 | solution.py:155
  162.5 2.6 %fusion.53 = bf16[5,512,512]{1,2,0:T(8,128)(2,1)S(1)} fusion(f32[512,512,5]{1,0,2:T(8,128)S(1)} %fusion.65, f32[5,512]{1,0:T(8,128)S(1)} %bitcast.243, f32[5,512]{1,0:T(8,128)} %bitcast.42, pred[512,512]{0,1:T(8,128)(4,1)S(1)} %iota_compare_fusion.3, bf16[512,1,5,128]{0,3,2,1:T(8,128)(2,1)S(1)} %copy-done.5, bf16[512,256]{1,0:T(8,128)(2,1)S(1)} %slice_bitcast_fusion.12), kind=kOutput, calls=%fused_computation.67 | convolution fusion | flops 343408640 | bytes 8939520 | tf_op jit(solution)/shard_map/cond/branch_1_fun/tgrd,ugd->grtu/dot_general | solution.py:81
  166.1 2.4 %fusion.59 = f32[512,128]{0,1:T(8,128)S(1)} fusion(f32[512,512,5]{1,0,2:T(8,128)S(1)} %fusion.65, f32[5,512]{1,0:T(8,128)} %bitcast.42, pred[512,512]{0,1:T(8,128)(4,1)S(1)} %iota_compare_fusion.3, bf16[512,1,5,128]{0,3,2,1:T(8,128)(2,1)S(1)} %copy-done.5), kind=kOutput, calls=%fused_computation.74 | convolution fusion | flops 340787200 | bytes 6432768 | tf_op jit(solution)/shard_map/cond/branch_1_fun/grtu,tgrd->ugd/dot_general | solution.py:87
  169.6 1.5 copy.54
  171.1 3.0 %fusion.57 = f32[512,1,5,128]{3,0,2,1:T(8,128)S(1)} fusion(f32[512,1,5,128]{3,0,2,1:T(8,128)} %copy.54, bf16[5,512,512]{1,2,0:T(8,128)(2,1)} %copy-done.2, bf16[512,256]{1,0:T(8,128)(2,1)S(1)} %copy-done.7), kind=kOutput, calls=%fused_computation.71 | convolution fusion | flops 335872000 | bytes 5373952 | tf_op jit(solution)/shard_map/cond/branch_1_fun/grtu,ugd->tgrd/dot_general | solution.py:83
  (113 shorter events, 27.4 us)
Async XLA Ops:
  7.2 63.7 %all-gather.2.cloned.1.call-start = ((), (), s32[]{:S(2)}) async-start(), calls=%async_computation.2 | async-start | bytes 6553600 | tf_op jit(solution)/shard_map/all_gather | solution.py:130
  7.9 169.7 %reduce-scatter.2.cloned.1.call-start = ((), (), s32[]{:S(2)}) async-start(), calls=%async_computation.1 | async-start | bytes 6553600 | tf_op jit(solution)/shard_map/reduce_scatter | solution.py:123
  15.7 6.5 %collective-permute-start = (bf16[512,256]{1,0:T(8,128)(2,1)S(1)}, bf16[512,256]{1,0:T(8,128)(2,1)S(1)}, u32[]{:S(2)}, u32[]{:S(2)}) collective-permute-start(bf16[512,256]{1,0:T(8,128)(2,1)S(1)} %get-tuple-element.865), channel_id=1, source_target_pairs={{0,4},{4,8},{8,12},{12,16},{16,20},{20,24},{24,28},{28,32},{32,36}... | collective-permute-start | bytes 786440 | tf_op jit(solution)/shard_map/while/body/eval_jaxpr/ppermute | solution.py:17
  22.3 7.7 %collective-permute-start = (bf16[512,256]{1,0:T(8,128)(2,1)S(1)}, bf16[512,256]{1,0:T(8,128)(2,1)S(1)}, u32[]{:S(2)}, u32[]{:S(2)}) collective-permute-start(bf16[512,256]{1,0:T(8,128)(2,1)S(1)} %get-tuple-element.865), channel_id=1, source_target_pairs={{0,4},{4,8},{8,12},{12,16},{16,20},{20,24},{24,28},{28,32},{32,36}... | collective-permute-start | bytes 786440 | tf_op jit(solution)/shard_map/while/body/eval_jaxpr/ppermute | solution.py:17
  30.0 7.7 %collective-permute-start = (bf16[512,256]{1,0:T(8,128)(2,1)S(1)}, bf16[512,256]{1,0:T(8,128)(2,1)S(1)}, u32[]{:S(2)}, u32[]{:S(2)}) collective-permute-start(bf16[512,256]{1,0:T(8,128)(2,1)S(1)} %get-tuple-element.865), channel_id=1, source_target_pairs={{0,4},{4,8},{8,12},{12,16},{16,20},{20,24},{24,28},{28,32},{32,36}... | collective-permute-start | bytes 786440 | tf_op jit(solution)/shard_map/while/body/eval_jaxpr/ppermute | solution.py:17
  60.1 22.4 %copy-start.3 = (f32[512,1,5,128]{0,3,2,1:T(8,128)S(1)}, f32[512,1,5,128]{0,3,2,1:T(8,128)}, u32[]{:S(2)}) copy-start(f32[512,1,5,128]{0,3,2,1:T(8,128)} %get-tuple-element.552) | copy-start | bytes 3932164
  94.1 19.4 %collective-permute-start.1 = (bf16[512,256]{0,1:T(8,128)(2,1)}, bf16[512,256]{0,1:T(8,128)(2,1)S(1)}, u32[]{:S(2)}, u32[]{:S(2)}) collective-permute-start(bf16[512,256]{0,1:T(8,128)(2,1)} %fusion.82), channel_id=1, source_target_pairs={{4,0},{8,4},{12,8},{16,12},{20,16},{24,20},{28,24},{32,28},{36,32}... | collective-permute-start | bytes 786440 | tf_op jit(solution)/shard_map/while/body/eval_jaxpr/ppermute | solution.py:17
  114.4 7.9 %copy-start = (bf16[512,256]{1,0:T(8,128)(2,1)}, bf16[512,256]{1,0:T(8,128)(2,1)S(1)}, u32[]{:S(2)}) copy-start(bf16[512,256]{1,0:T(8,128)(2,1)S(1)} %dynamic-slice_bitcast_fusion.2) | copy-start | bytes 786436 | tf_op jit(solution)/shard_map/while/body/eval_jaxpr/cond
  117.5 5.7 %slice-start = ((s8[5242880]{0:T(1024)(128)(4,1)}), s8[4194304]{0:T(1024)(128)(4,1)S(1)}, s32[]{:S(2)}) async-start(s8[5242880]{0:T(1024)(128)(4,1)} %bitcast.231), calls=%async_computation.3 | async-start | bytes 8388608 | tf_op jit(solution)/shard_map/while/body/eval_jaxpr/cond
  117.6 5.7 %slice-start.1 = ((s8[5242880]{0:T(1024)(128)(4,1)}), s8[1048576]{0:T(1024)(128)(4,1)S(1)}, s32[]{:S(2)}) async-start(s8[5242880]{0:T(1024)(128)(4,1)} %bitcast.231), calls=%async_computation.4 | async-start | bytes 2097152 | tf_op jit(solution)/shard_map/while/body/eval_jaxpr/cond
  117.6 5.7 %copy-start.4 = (bf16[512,1,5,128]{0,3,2,1:T(8,128)(2,1)S(1)}, bf16[512,1,5,128]{0,3,2,1:T(8,128)(2,1)}, u32[]{:S(2)}) copy-start(bf16[512,1,5,128]{0,3,2,1:T(8,128)(2,1)} %get-tuple-element.517) | copy-start | bytes 1966084 | tf_op jit(solution)/shard_map/while/body/eval_jaxpr/cond
  123.3 2.5 %copy-start.1 = (bf16[512,256]{1,0:T(8,128)(2,1)S(1)}, bf16[512,256]{1,0:T(8,128)(2,1)}, u32[]{:S(2)}) copy-start(bf16[512,256]{1,0:T(8,128)(2,1)} %copy-done) | copy-start | bytes 786436 | tf_op jit(solution)/shard_map/while/body/eval_jaxpr/cond
  128.3 8.3 %collective-permute-start.1 = (bf16[512,256]{0,1:T(8,128)(2,1)}, bf16[512,256]{0,1:T(8,128)(2,1)S(1)}, u32[]{:S(2)}, u32[]{:S(2)}) collective-permute-start(bf16[512,256]{0,1:T(8,128)(2,1)} %fusion.82), channel_id=1, source_target_pairs={{4,0},{8,4},{12,8},{16,12},{20,16},{24,20},{28,24},{32,28},{36,32}... | collective-permute-start | bytes 786440 | tf_op jit(solution)/shard_map/while/body/eval_jaxpr/ppermute | solution.py:17
  137.4 7.8 %copy-start = (bf16[512,256]{1,0:T(8,128)(2,1)}, bf16[512,256]{1,0:T(8,128)(2,1)S(1)}, u32[]{:S(2)}) copy-start(bf16[512,256]{1,0:T(8,128)(2,1)S(1)} %dynamic-slice_bitcast_fusion.2) | copy-start | bytes 786436 | tf_op jit(solution)/shard_map/while/body/eval_jaxpr/cond
  140.6 5.7 %slice-start = ((s8[5242880]{0:T(1024)(128)(4,1)}), s8[4194304]{0:T(1024)(128)(4,1)S(1)}, s32[]{:S(2)}) async-start(s8[5242880]{0:T(1024)(128)(4,1)} %bitcast.231), calls=%async_computation.3 | async-start | bytes 8388608 | tf_op jit(solution)/shard_map/while/body/eval_jaxpr/cond
  140.7 5.6 %slice-start.1 = ((s8[5242880]{0:T(1024)(128)(4,1)}), s8[1048576]{0:T(1024)(128)(4,1)S(1)}, s32[]{:S(2)}) async-start(s8[5242880]{0:T(1024)(128)(4,1)} %bitcast.231), calls=%async_computation.4 | async-start | bytes 2097152 | tf_op jit(solution)/shard_map/while/body/eval_jaxpr/cond
  140.7 5.6 %copy-start.4 = (bf16[512,1,5,128]{0,3,2,1:T(8,128)(2,1)S(1)}, bf16[512,1,5,128]{0,3,2,1:T(8,128)(2,1)}, u32[]{:S(2)}) copy-start(bf16[512,1,5,128]{0,3,2,1:T(8,128)(2,1)} %get-tuple-element.517) | copy-start | bytes 1966084 | tf_op jit(solution)/shard_map/while/body/eval_jaxpr/cond
  146.3 2.5 %copy-start.1 = (bf16[512,256]{1,0:T(8,128)(2,1)S(1)}, bf16[512,256]{1,0:T(8,128)(2,1)}, u32[]{:S(2)}) copy-start(bf16[512,256]{1,0:T(8,128)(2,1)} %copy-done) | copy-start | bytes 786436 | tf_op jit(solution)/shard_map/while/body/eval_jaxpr/cond
  151.3 7.9 %collective-permute-start.1 = (bf16[512,256]{0,1:T(8,128)(2,1)}, bf16[512,256]{0,1:T(8,128)(2,1)S(1)}, u32[]{:S(2)}, u32[]{:S(2)}) collective-permute-start(bf16[512,256]{0,1:T(8,128)(2,1)} %fusion.82), channel_id=1, source_target_pairs={{4,0},{8,4},{12,8},{16,12},{20,16},{24,20},{28,24},{32,28},{36,32}... | collective-permute-start | bytes 786440 | tf_op jit(solution)/shard_map/while/body/eval_jaxpr/ppermute | solution.py:17
  161.3 1.2 copy-start.5
  161.3 3.8 %copy-start.6 = (bf16[512,256]{1,0:T(8,128)(2,1)}, bf16[512,256]{1,0:T(8,128)(2,1)S(1)}, u32[]{:S(2)}) copy-start(bf16[512,256]{1,0:T(8,128)(2,1)S(1)} %slice_bitcast_fusion.12) | copy-start | bytes 786436 | tf_op jit(solution)/shard_map/cond
  165.1 3.4 %copy-start.2 = (bf16[5,512,512]{1,2,0:T(8,128)(2,1)}, bf16[5,512,512]{1,2,0:T(8,128)(2,1)S(1)}, u32[]{:S(2)}) copy-start(bf16[5,512,512]{1,2,0:T(8,128)(2,1)S(1)} %fusion.53) | copy-start | bytes 7864324 | tf_op jit(solution)/shard_map/cond
  166.1 5.0 %copy-start.7 = (bf16[512,256]{1,0:T(8,128)(2,1)S(1)}, bf16[512,256]{1,0:T(8,128)(2,1)}, u32[]{:S(2)}) copy-start(bf16[512,256]{1,0:T(8,128)(2,1)} %copy-done.6) | copy-start | bytes 786436 | tf_op jit(solution)/shard_map/cond
Sparse Core Ops, SparseCore 0:
  9.8 61.0 all-gather.1
  92.9 58.4 reduce-scatter.1
where the time goes:
time: 185 us; the launch traced here: 184 us
  matrix products  67.7 us (37%)
  waiting for transfers between devices  50.4 us (27%)
  starting transfers between devices  18.4 us (10%)
  other arithmetic  17.4 us (9%)
  between operations  14.8 us (8%)
  local copies, waits for them, and re-layouts  14.5 us (8%)
    ppermute x6, waiting for transfers between devices, from_behind(): return lax.ppermute(x, axis, pairs)  39 us
    ppermute x6, starting transfers between devices, from_behind(): return lax.ppermute(x, axis, pairs)  18.4 us
    dot_general x3, matrix products, live(): jnp.einsum('grtu,ugd->tgrd', weights, value_blk, preferred_element_type=j...  12.9 us
    dot_general x3, matrix products, task_grads(): jnp.einsum('tgrd,ugd->grtu', grad_blk, value_blk, preferred_element_type=...  11.8 us
    all_gather x1, waiting for transfers between devices, on_device(): lax.all_gather(grad_output, 'tp', axis=0, tiled=True)  10.7 us
    dot_general x6, matrix products, masked_scores(): jnp.einsum('tgrd,ugd->grtu', query_blk, key_blk, preferred_element_type=j...  10.2 us
    dot_general x1, matrix products, on_device(): lax.dot_general(lax.all_gather(grad_output, 'tp', axis=0, tiled=True), ou...  9.52 us
    dot_general x1, matrix products, on_device(): jnp.dot(attn_out, out_weight, preferred_element_type=jnp.float32)  8.9 us
  transfers between devices with their start and end apart: 8, of which 7 were waited for; matrix products, arithmetic and copies ran while one was open for 42% of the time, Pallas kernels for 0%

commit v1 on v0

v1 whole, which is shorter than its diff:
```python
import functools

import jax
import jax.numpy as jnp
from jax import lax
from jax.experimental import pallas as pl
from jax.experimental.pallas import tpu as pltpu
from jax.sharding import PartitionSpec as P

HD = 128
REACH = 4
GROUP = 5
N_TP = 4
PARTS = 8
CHUNKS = 4
NEGATIVE = -1e30
SCALE = HD ** (-0.5)
LOG2E = 1.4426950408889634
MESH = pl.DeviceIdType.MESH
BF, F32 = jnp.bfloat16, jnp.float32


def dot(a, b):
    return jnp.dot(a, b, preferred_element_type=F32)


def dot_nt(a, b):
    return lax.dot_general(a, b, (((1,), (1,)), ((), ())), preferred_element_type=F32)


def kernel(
    n,
    docs,
    len_ref,
    q_ref,
    k_ref,
    v_ref,
    w_ref,
    go_ref,
    lo_ref,
    gq_ref,
    gk_ref,
    gv_ref,
    qh,
    qt,
    kb,
    vb,
    kt,
    vt,
    wm,
    wp,
    go,
    acc,
    stat_m,
    stat_l,
    ot,
    o_all,
    op,
    rs_send,
    rs_recv,
    lo_acc,
    lo_out,
    dot_acc,
    dot_own,
    dot_rem,
    dot_send,
    d_own,
    d_rem,
    delta,
    dk_acc,
    dv_acc,
    dq_acc,
    dkv_send,
    dkv_recv,
    gq_out,
    gk_out,
    gv_out,
    tabs_ref,
    loc_sem,
    out_sem,
    send_sem,
    recv_sem,
):
    tok, width = q_ref.shape
    row = tok // N_TP
    two = 2 * row
    feat = go_ref.shape[1]
    half = feat // 2
    me, y = lax.axis_index("attn"), lax.axis_index("tp")
    step_x = n // 4
    core = lax.rem(me, 2)
    x = me // step_x
    y_a = y + 1 - 2 * lax.rem(y, 2)
    y_b = N_TP - 1 - y
    perm = [y, y_b, y_a, N_TP - 1 - y_a]

    def at(shift):
        return (lax.rem(me + shift + n, n), y)

    dev_a, dev_b = (me, y_a), (me, y_b)
    x_up, x_down = at(step_x), at(-step_x)
    sib = (me + 1 - 2 * core, y)

    def part_of(shift):
        return lax.rem(x + shift + 4, 4) * 2 + core

    partners = [at(s) for s in (1, 2, 3, -1, -2, -3)] + [dev_a, dev_b, x_up, x_down]
    barrier = pltpu.get_barrier_semaphore()
    for dev in partners:
        pl.semaphore_signal(barrier, inc=1, device_id=dev, device_id_type=MESH)

    def local(i, src, dst):
        c = pltpu.make_async_copy(src, dst, loc_sem.at[i])
        c.start()
        return c

    loc_k = local(0, k_ref, kb.at[0])
    loc_v = local(1, v_ref, vb.at[0])
    loc_q = []
    for s in range(N_TP):
        rows = pl.ds(pl.multiple_of(perm[s] * row, row), row)
        for h in range(GROUP):
            loc_q.append(
                local(
                    2 + s * GROUP + h,
                    q_ref.at[rows, pl.ds(h * HD, HD)],
                    qh.at[h, pl.ds(s * row, row)],
                )
            )
    loc_go = local(2 + N_TP * GROUP, go_ref, go.at[0])
    loc_w = local(3 + N_TP * GROUP, w_ref, wm)

    pl.semaphore_wait(barrier, len(partners))

    used = [0]

    def remote(src, dst, dev):
        i = used[0]
        used[0] += 1
        c = pltpu.make_async_remote_copy(
            src_ref=src,
            dst_ref=dst,
            send_sem=send_sem.at[i],
            recv_sem=recv_sem.at[i],
            device_id=dev,
            device_id_type=MESH,
        )
        c.start()
        return c

    sides = [pl.ds(0, half), pl.ds(half, half)]
    mine = part_of(0)
    kv = [None]
    kv.append((remote(k_ref, kb.at[1], at(1)), remote(v_ref, vb.at[1], at(1))))
    wa = [remote(w_ref.at[mine, :, sides[0]], wp.at[mine, :, sides[0]], dev_a)]
    kv.append((remote(k_ref, kb.at[2], at(2)), remote(v_ref, vb.at[2], at(2))))
    kv.append((remote(k_ref, kb.at[3], at(3)), remote(v_ref, vb.at[3], at(3))))
    wa.append(remote(w_ref.at[mine, :, sides[1]], wp.at[mine, :, sides[1]], dev_a))
    go_b = remote(go_ref, go.at[1], dev_b)

    end, first = jnp.int32(0), jnp.int32(0)
    for d in range(docs):
        end = end + len_ref[d]
        first = jnp.where(end <= me, end, first)
    depth = me - first
    bias = [jnp.where(o <= depth, 0.0, -NEGATIVE).astype(F32) for o in range(REACH)]

    lane = lax.broadcasted_iota(jnp.int32, (1, row), 1)
    for s in range(N_TP):
        tabs_ref[:, s * row : (s + 1) * row] = lane + perm[s] * row

    c2 = SCALE * LOG2E

    for c in loc_q:
        c.wait()

    def turn_q(h, carry):
        qt[h] = qh[h].T
        return carry

    lax.fori_loop(0, GROUP, turn_q, 0)

    def turn_kv(o):
        kt[o] = kb[o].T
        vt[o] = vb[o].T

    def forward(o):
        turn_kv(o)

        def head(h, carry):
            s = dot(kb[o], qt[h])
            if o == 0:
                at_u = lax.broadcasted_iota(jnp.int32, (tok, tok), 0)
                s = jnp.where(at_u <= tabs_ref[...], s, NEGATIVE)
                new = jnp.max(s, axis=0, keepdims=True)
                p = jnp.exp2((s - new) * c2)
                stat_l[h] = jnp.sum(p, axis=0, keepdims=True)
                acc[h] = dot(vt[o], p.astype(BF))
            else:
                old = stat_m[h]
                new = jnp.maximum(old, jnp.max(s, axis=0, keepdims=True) - bias[o])
                fade = jnp.exp2((old - new) * c2)
                p = jnp.exp2((s - (new + bias[o])) * c2)
                stat_l[h] = stat_l[h] * fade + jnp.sum(p, axis=0, keepdims=True)
                acc[h] = acc[h] * fade + dot(vt[o], p.astype(BF))
            stat_m[h] = new
            return carry

        lax.fori_loop(0, GROUP, head, 0)

    loc_k.wait()
    loc_v.wait()
    forward(0)
    for c in kv[1]:
        c.wait_recv()
    forward(1)

    wa[0].wait_recv()
    piece = wp.at[mine, :, sides[0]]
    up0 = remote(piece, piece, x_up)
    down0 = remote(piece, piece, x_down)
    sibs = [remote(piece, piece, sib)]

    for c in kv[2]:
        c.wait_recv()
    forward(2)

    wa[1].wait_recv()
    piece = wp.at[mine, :, sides[1]]
    up1 = remote(piece, piece, x_up)
    down1 = remote(piece, piece, x_down)
    sibs.append(remote(piece, piece, sib))

    for c in kv[3]:
        c.wait_recv()
    forward(3)

    for h in range(GROUP):
        low = (acc[h] * (1.0 / stat_l[h])).astype(BF)
        ot[h] = low
        o_all[:, h * HD : (h + 1) * HD] = low.T
        stat_l[h] = stat_m[h] * c2 + jnp.log2(stat_l[h])
    o_a = remote(o_all.at[pl.ds(two, two)], op, dev_a)

    from_down, from_up, from_far = part_of(-1), part_of(1), part_of(2)
    up0.wait_recv()
    piece = wp.at[from_down, :, sides[0]]
    far_up = remote(piece, piece, x_up)
    sibs.append(remote(piece, piece, sib))
    down0.wait_recv()
    piece = wp.at[from_up, :, sides[0]]
    sibs.append(remote(piece, piece, sib))

    def cotangent(w3, out):
        dot_acc[...] = jnp.zeros_like(dot_acc)
        deep = feat // CHUNKS

        def step(j, carry):
            cols = pl.ds(pl.multiple_of(j * deep, deep), deep)
            part = w3[:, :, cols].reshape(width, deep)
            for s in range(2):
                dot_acc[:, s * row : (s + 1) * row] += dot_nt(part, go[s, :, cols])
            return carry

        lax.fori_loop(0, CHUNKS, step, 0)
        for h in range(GROUP):
            out[h] = dot_acc[h * HD : (h + 1) * HD, :].astype(BF)

    def turn_d(src, dst, base):
        def head(h, carry):
            high = src[h]
            dst[h] = high.T
            delta[h, :, pl.ds(base, two)] = jnp.sum(
                high.astype(F32) * ot[h, :, pl.ds(base, two)].astype(F32), axis=0, keepdims=True
            )
            return carry

        lax.fori_loop(0, GROUP, head, 0)

    loc_w.wait()
    loc_go.wait()
    go_b.wait_recv()
    cotangent(wm, dot_own)
    turn_d(dot_own, d_own, 0)

    up1.wait_recv()
    piece = wp.at[from_down, :, sides[1]]
    sibs.append(remote(piece, piece, sib))
    down1.wait_recv()
    piece = wp.at[from_up, :, sides[1]]
    far_down = remote(piece, piece, x_down)
    sibs.append(remote(piece, piece, sib))

    def backward(o, base, dt, dd, fresh):
        tl = pl.ds(base, two)

        def head(h, carry):
            s = dot(kb[o], qt[h, :, tl])
            p = jnp.exp2(s * c2 - (stat_l[h, :, tl] + bias[o]))
            if o == 0:
                at_u = lax.broadcasted_iota(jnp.int32, (tok, two), 0)
                p = jnp.where(at_u <= tabs_ref[:, tl], p, 0.0)
            dp = dot(vb[o], dt[h])
            ds = (p * (dp - delta[h, :, tl])).astype(BF)
            dv_acc[o] += dot(p.astype(BF), dd[h])
            dk_acc[o] += dot(ds, qh[h, tl])
            part_q = dot(kt[o], ds)
            if o == REACH - 1:
                dq_acc[h, :, tl] = part_q
            else:
                dq_acc[h, :, tl] += part_q
            return carry

        if fresh:
            dv_acc[o] = jnp.zeros((tok, HD), F32)
            dk_acc[o] = jnp.zeros((tok, HD), F32)
        lax.fori_loop(0, GROUP, head, 0)

    for o in range(REACH - 1, -1, -1):
        backward(o, 0, dot_own, d_own, True)

    far_up.wait_recv()
    piece = wp.at[from_far, :, sides[0]]
    sibs.append(remote(piece, piece, sib))
    far_down.wait_recv()
    piece = wp.at[from_far, :, sides[1]]
    sibs.append(remote(piece, piece, sib))
    for c in sibs:
        c.wait_recv()
    o_a.wait_recv()

    wide = feat // CHUNKS
    rs = []
    for j in range(CHUNKS):
        cols = slice(j * wide, (j + 1) * wide)
        one = dot(o_all[0:two], wm[:, :, cols].reshape(width, wide)).astype(BF)
        other = dot(op[...], wp[:, :, cols].reshape(width, wide)).astype(BF)
        both = one.astype(F32) + other.astype(F32)
        lo_acc[:, cols] = both[0:row]
        rs_send[:, cols] = both[row:two].astype(BF)
        span = pl.ds(j * wide, wide)
        rs.append(remote(rs_send.at[:, span], rs_recv.at[:, span], dev_b))

    cotangent(wp, dot_send)
    d_a = remote(dot_send, dot_rem, dev_a)
    d_a.wait_recv()
    turn_d(dot_rem, d_rem, two)

    back = []
    for o in range(REACH - 1, -1, -1):
        backward(o, two, dot_rem, d_rem, False)
        if o > 0:
            dkv_send[o - 1, :, 0:HD] = (dk_acc[o] * SCALE).astype(BF)
            dkv_send[o - 1, :, HD : 2 * HD] = dv_acc[o].astype(BF)
            back.append(remote(dkv_send.at[o - 1], dkv_recv.at[o - 1], at(-o)))

    outs = []

    def put(src, dst):
        c = pltpu.make_async_copy(src, dst, out_sem.at[len(outs)])
        c.start()
        outs.append(c)

    for h in range(GROUP):
        gq_out[:, h * HD : (h + 1) * HD] = (dq_acc[h] * SCALE).T.astype(BF)
    for s in range(N_TP):
        rows = pl.ds(pl.multiple_of(perm[s] * row, row), row)
        put(gq_out.at[pl.ds(s * row, row)], gq_ref.at[rows])

    for c in rs:
        c.wait_recv()
    lo_out[...] = (lo_acc[...] + rs_recv[...].astype(F32)).astype(BF)
    put(lo_out, lo_ref)

    for c in back:
        c.wait_recv()
    gk = dk_acc[0] * SCALE
    gv = dv_acc[0]
    for o in range(1, REACH):
        gk = gk + dkv_recv[o - 1, :, 0:HD].astype(F32)
        gv = gv + dkv_recv[o - 1, :, HD : 2 * HD].astype(F32)
    gk_out[...] = gk.astype(BF)
    gv_out[...] = gv.astype(BF)
    put(gk_out, gk_ref)
    put(gv_out, gv_ref)

    sent = [c for pair in kv[1:] for c in pair] + wa + [go_b, up0, down0, up1, down1]
    sent += sibs + [far_up, far_down, o_a, d_a] + rs + back
    for c in sent:
        c.wait_send()
    for c in outs:
        c.wait()


def on_device(n, lengths, queries, key_vectors, value_vectors, out_weight, grad_output):
    tok, width = queries.shape
    feat = out_weight.shape[1]
    row, two = tok // N_TP, tok // 2
    docs = lengths.shape[0]
    hbm = pl.BlockSpec(memory_space=pl.ANY)
    vm = pltpu.VMEM
    dma = pltpu.SemaphoreType.DMA
    flops = 2 * tok * width * feat * 2 + 7 * 2 * tok * tok * width * REACH
    return pl.pallas_call(
        functools.partial(kernel, n, docs),
        out_shape=(
            jax.ShapeDtypeStruct((row, feat), BF),
            jax.ShapeDtypeStruct((tok, width), BF),
            jax.ShapeDtypeStruct((tok, HD), BF),
            jax.ShapeDtypeStruct((tok, HD), BF),
        ),
        in_specs=[pl.BlockSpec(memory_space=pltpu.SMEM)] + [hbm] * 5,
        out_specs=(hbm,) * 4,
        scratch_shapes=[
            vm((GROUP, tok, HD), BF),
            vm((GROUP, HD, tok), BF),
            vm((REACH, tok, HD), BF),
            vm((REACH, tok, HD), BF),
            vm((REACH, HD, tok), BF),
            vm((REACH, HD, tok), BF),
            vm((PARTS, width // PARTS, feat), BF),
            vm((PARTS, width // PARTS, feat), BF),
            vm((2, row, feat), BF),
            vm((GROUP, HD, tok), F32),
            vm((GROUP, 1, tok), F32),
            vm((GROUP, 1, tok), F32),
            vm((GROUP, HD, tok), BF),
            vm((tok, width), BF),
            vm((two, width), BF),
            vm((row, feat), BF),
            vm((row, feat), BF),
            vm((row, feat), F32),
            vm((row, feat), BF),
            vm((width, two), F32),
            vm((GROUP, HD, two), BF),
            vm((GROUP, HD, two), BF),
            vm((GROUP, HD, two), BF),
            vm((GROUP, two, HD), BF),
            vm((GROUP, two, HD), BF),
            vm((GROUP, 1, tok), F32),
            vm((REACH, tok, HD), F32),
            vm((REACH, tok, HD), F32),
            vm((GROUP, HD, tok), F32),
            vm((REACH - 1, tok, 2 * HD), BF),
            vm((REACH - 1, tok, 2 * HD), BF),
            vm((tok, width), BF),
            vm((tok, HD), BF),
            vm((tok, HD), BF),
            vm((1, tok), jnp.int32),
            dma((4 + N_TP * GROUP,)),
            dma((7,)),
            dma((40,)),
            dma((40,)),
        ],
        compiler_params=pltpu.CompilerParams(
            collective_id=0, has_side_effects=True, vmem_limit_bytes=56 * 1024 * 1024
        ),
        cost_estimate=pl.CostEstimate(flops=flops, bytes_accessed=1 << 24, transcendentals=1 << 23),
    )(
        lengths,
        queries,
        key_vectors,
        value_vectors,
        out_weight.reshape(PARTS, width // PARTS, feat),
        grad_output,
    )


def solution(mesh):
    return jax.shard_map(
        functools.partial(on_device, mesh.shape["attn"]),
        mesh=mesh,
        in_specs=(
            P(),
            P("attn", "tp"),
            P("attn", "tp"),
            P("attn", "tp"),
            P("tp", None),
            P(("attn", "tp"), None),
        ),
        out_specs=(P(("attn", "tp"), None), P("attn", "tp"), P("attn", "tp"), P("attn", "tp")),
        check_vma=False,
    )
```

time: 185 us -> 101 us (0.55)
  the two profiles are of different devices: /device:TPU:135 before, /device:TPU:75 now
where the time goes in v1:
time: 101 us
  Pallas kernels  95.6 us (95%)
  local copies, waits for them, and re-layouts  4.84 us (5%)
    pallas_call x1, Pallas kernels, on_device(): pl.pallas_call(functools.partial(kernel, n, docs), out_shape=(jax.ShapeDt...  95.6 us
    unnamed x10, local copies, waits for them, and re-layouts  4.84 us

profile of v1, /device:TPU:75, one launch (start us, length us, event | category | flops | bytes accessed | tf_op | source)
XLA Modules:
  0.0 101.0 jit_solution(6933727916427154699)
XLA Ops:
  0.6 95.6 %shard_map.93 = (bf16[128,5120]{1,0:T(8,128)(2,1)}, bf16[512,640]{1,0:T(8,128)(2,1)}, bf16[512,128]{1,0:T(8,128)(2,1)}, bf16[512,128]{1,0:T(8,128)(2,1)}) custom-call(s32[32]{0:T(128)} %len_ref.1, bf16[512,640]{1,0:T(8,128)(2,1)} %q_ref.1, bf16[512,128]{1,0:T(8,128)(2,1)} %k_ref.1, bf16[512,128]{1,0:T(8,128)(2,1)} %v_ref.1, bf16[8,80,5120]{2,1,0:T(8,128)(2,1)} %bitcast.1, ...), custom_call_target="tpu_custom_call" | custom-call | flops 16106127360 | bytes 16777216 | tf_op jit(solution)/shard_map/pallas_call | solution.py:404
  96.2 0.0 copy-start
  96.2 2.5 %copy.14 = bf16[128,5120]{1,0:T(8,128)(2,1)} copy(bf16[128,5120]{1,0:T(8,128)(2,1)} %get-tuple-element.8) | data formatting | bytes 2621440
  98.7 0.0 copy-done
  98.7 0.0 copy-start.2
  98.7 0.0 copy-start.1
  98.7 0.8 copy.15
  99.6 0.2 copy-done.2
  99.7 0.7 copy.16
  100.4 0.0 copy-done.1
  100.4 0.7 copy.17
Async XLA Ops:
  96.2 2.5 %copy-start = (bf16[512,640]{1,0:T(8,128)(2,1)S(1)}, bf16[512,640]{1,0:T(8,128)(2,1)}, u32[]{:S(2)}) copy-start(bf16[512,640]{1,0:T(8,128)(2,1)} %get-tuple-element.9) | copy-start | bytes 1966084
  98.7 1.0 copy-start.2
  98.7 1.7 %copy-start.1 = (bf16[512,128]{1,0:T(8,128)(2,1)S(1)}, bf16[512,128]{1,0:T(8,128)(2,1)}, u32[]{:S(2)}) copy-start(bf16[512,128]{1,0:T(8,128)(2,1)} %get-tuple-element.11) | copy-start | bytes 393220

commit v2 on v1

--- a/solution.py
+++ b/solution.py
@@ -61,6 +61,7 @@
     lo_acc,
     lo_out,
     dot_acc,
+    dot_acc_a,
     dot_own,
     dot_rem,
     dot_send,
@@ -85,7 +86,6 @@
     row = tok // N_TP
     two = 2 * row
     feat = go_ref.shape[1]
-    half = feat // 2
     me, y = lax.axis_index("attn"), lax.axis_index("tp")
     step_x = n // 4
     core = lax.rem(me, 2)
@@ -148,15 +148,56 @@
         c.start()
         return c
 
-    sides = [pl.ds(0, half), pl.ds(half, half)]
-    mine = part_of(0)
-    kv = [None]
-    kv.append((remote(k_ref, kb.at[1], at(1)), remote(v_ref, vb.at[1], at(1))))
-    wa = [remote(w_ref.at[mine, :, sides[0]], wp.at[mine, :, sides[0]], dev_a)]
-    kv.append((remote(k_ref, kb.at[2], at(2)), remote(v_ref, vb.at[2], at(2))))
-    kv.append((remote(k_ref, kb.at[3], at(3)), remote(v_ref, vb.at[3], at(3))))
-    wa.append(remote(w_ref.at[mine, :, sides[1]], wp.at[mine, :, sides[1]], dev_a))
-    go_b = remote(go_ref, go.at[1], dev_b)
+    wide = feat // CHUNKS
+    cols = [pl.ds(j * wide, wide) for j in range(CHUNKS)]
+    mine, from_down, from_up, from_far = [part_of(s) for s in (0, -1, 1, 2)]
+    kv = [None, (remote(k_ref, kb.at[1], at(1)), remote(v_ref, vb.at[1], at(1)))]
+    wa, go_b = [], []
+    for j in range(CHUNKS):
+        wa.append(remote(w_ref.at[mine, :, cols[j]], wp.at[mine, :, cols[j]], dev_a))
+        go_b.append(remote(go_ref.at[:, cols[j]], go.at[1, :, cols[j]], dev_b))
+
+    up, down, far = {}, {}, {}
+    sibs = [[] for _ in range(CHUNKS)]
+
+    def pass_own(j):
+        wa[j].wait_recv()
+        piece = wp.at[mine, :, cols[j]]
+        up[j] = remote(piece, piece, x_up)
+        down[j] = remote(piece, piece, x_down)
+        sibs[j].append(remote(piece, piece, sib))
+
+    def pass_near(j):
+        up[j].wait_recv()
+        piece = wp.at[from_down, :, cols[j]]
+        if j % 2 == 0:
+            far[j] = remote(piece, piece, x_up)
+        sibs[j].append(remote(piece, piece, sib))
+        down[j].wait_recv()
+        piece = wp.at[from_up, :, cols[j]]
+        if j % 2 == 1:
+            far[j] = remote(piece, piece, x_down)
+        sibs[j].append(remote(piece, piece, sib))
+
+    def pass_far(j):
+        far[j].wait_recv()
+        piece = wp.at[from_far, :, cols[j]]
+        sibs[j].append(remote(piece, piece, sib))
+
+    def have(j):
+        for c in sibs[j]:
+            c.wait_recv()
+
+    def next_keys(o):
+        for c in kv[o]:
+            c.wait_recv()
+        if o < REACH - 1:
+            kv.append(
+                (
+                    remote(kb.at[o], kb.at[o + 1], at(1)),
+                    remote(vb.at[o], vb.at[o + 1], at(1)),
+                )
+            )
 
     end, first = jnp.int32(0), jnp.int32(0)
     for d in range(docs):
@@ -211,28 +252,13 @@
     loc_k.wait()
     loc_v.wait()
     forward(0)
-    for c in kv[1]:
-        c.wait_recv()
+    next_keys(1)
     forward(1)
-
-    wa[0].wait_recv()
-    piece = wp.at[mine, :, sides[0]]
-    up0 = remote(piece, piece, x_up)
-    down0 = remote(piece, piece, x_down)
-    sibs = [remote(piece, piece, sib)]
-
-    for c in kv[2]:
-        c.wait_recv()
+    pass_own(0)
+    next_keys(2)
     forward(2)
-
-    wa[1].wait_recv()
-    piece = wp.at[mine, :, sides[1]]
-    up1 = remote(piece, piece, x_up)
-    down1 = remote(piece, piece, x_down)
-    sibs.append(remote(piece, piece, sib))
-
-    for c in kv[3]:
-        c.wait_recv()
+    pass_own(1)
+    next_keys(3)
     forward(3)
 
     for h in range(GROUP):
@@ -242,29 +268,30 @@
         stat_l[h] = stat_m[h] * c2 + jnp.log2(stat_l[h])
     o_a = remote(o_all.at[pl.ds(two, two)], op, dev_a)
 
-    from_down, from_up, from_far = part_of(-1), part_of(1), part_of(2)
-    up0.wait_recv()
-    piece = wp.at[from_down, :, sides[0]]
-    far_up = remote(piece, piece, x_up)
-    sibs.append(remote(piece, piece, sib))
-    down0.wait_recv()
-    piece = wp.at[from_up, :, sides[0]]
-    sibs.append(remote(piece, piece, sib))
-
-    def cotangent(w3, out):
-        dot_acc[...] = jnp.zeros_like(dot_acc)
-        deep = feat // CHUNKS
-
-        def step(j, carry):
-            cols = pl.ds(pl.multiple_of(j * deep, deep), deep)
-            part = w3[:, :, cols].reshape(width, deep)
-            for s in range(2):
-                dot_acc[:, s * row : (s + 1) * row] += dot_nt(part, go[s, :, cols])
-            return carry
-
-        lax.fori_loop(0, CHUNKS, step, 0)
+    def cotangent(w3, total, j):
+        part = dot_nt(
+            w3[:, :, cols[j]].reshape(width, wide), go[:, :, cols[j]].reshape(two, wide)
+        )
+        if j == 0:
+            total[...] = part
+        else:
+            total[...] += part
+
+    def heads_of(total, out):
         for h in range(GROUP):
-            out[h] = dot_acc[h * HD : (h + 1) * HD, :].astype(BF)
+            out[h] = total[h * HD : (h + 1) * HD, :].astype(BF)
+
+    rs = []
+
+    def project(j):
+        one = dot(o_all[0:two], wm[:, :, cols[j]].reshape(width, wide)).astype(BF)
+        other = dot(op[...], wp[:, :, cols[j]].reshape(width, wide)).astype(BF)
+        both = one.astype(F32) + other.astype(F32)
+        lo_acc[:, cols[j]] = both[0:row]
+        rs_send[:, cols[j]] = both[row:two].astype(BF)
+
+    def send_rows(j):
+        rs.append(remote(rs_send.at[:, cols[j]], rs_recv.at[:, cols[j]], dev_b))
 
     def turn_d(src, dst, base):
         def head(h, carry):
@@ -277,19 +304,47 @@
 
         lax.fori_loop(0, GROUP, head, 0)
 
+    pass_near(0)
+    pass_near(1)
+    pass_own(2)
     loc_w.wait()
     loc_go.wait()
-    go_b.wait_recv()
-    cotangent(wm, dot_own)
+    go_b[0].wait_recv()
+    cotangent(wm, dot_acc, 0)
+    go_b[1].wait_recv()
+    cotangent(wm, dot_acc, 1)
+    pass_own(3)
+    pass_far(0)
+    pass_far(1)
+    have(0)
+    have(1)
+    cotangent(wp, dot_acc_a, 0)
+    cotangent(wp, dot_acc_a, 1)
+    o_a.wait_recv()
+    project(0)
+    project(1)
+    pass_near(2)
+    go_b[2].wait_recv()
+    cotangent(wm, dot_acc, 2)
+    pass_near(3)
+    go_b[3].wait_recv()
+    send_rows(0)
+    send_rows(1)
+    cotangent(wm, dot_acc, 3)
+    heads_of(dot_acc, dot_own)
     turn_d(dot_own, d_own, 0)
-
-    up1.wait_recv()
-    piece = wp.at[from_down, :, sides[1]]
-    sibs.append(remote(piece, piece, sib))
-    down1.wait_recv()
-    piece = wp.at[from_up, :, sides[1]]
-    far_down = remote(piece, piece, x_down)
-    sibs.append(remote(piece, piece, sib))
+    pass_far(2)
+    pass_far(3)
+    have(2)
+    have(3)
+    cotangent(wp, dot_acc_a, 2)
+    cotangent(wp, dot_acc_a, 3)
+    heads_of(dot_acc_a, dot_send)
+    d_a = remote(dot_send, dot_rem, dev_a)
+    project(2)
+    send_rows(2)
+    project(3)
+    send_rows(3)
 
     def backward(o, base, dt, dd, fresh):
         tl = pl.ds(base, two)
@@ -316,43 +371,41 @@
             dk_acc[o] = jnp.zeros((tok, HD), F32)
         lax.fori_loop(0, GROUP, head, 0)
 
-    for o in range(REACH - 1, -1, -1):
+    def own_rows(o):
         backward(o, 0, dot_own, d_own, True)
 
-    far_up.wait_recv()
-    piece = wp.at[from_far, :, sides[0]]
-    sibs.append(remote(piece, piece, sib))
-    far_down.wait_recv()
-    piece = wp.at[from_far, :, sides[1]]
-    sibs.append(remote(piece, piece, sib))
-    for c in sibs:
-        c.wait_recv()
-    o_a.wait_recv()
-
-    wide = feat // CHUNKS
-    rs = []
-    for j in range(CHUNKS):
-        cols = slice(j * wide, (j + 1) * wide)
-        one = dot(o_all[0:two], wm[:, :, cols].reshape(width, wide)).astype(BF)
-        other = dot(op[...], wp[:, :, cols].reshape(width, wide)).astype(BF)
-        both = one.astype(F32) + other.astype(F32)
-        lo_acc[:, cols] = both[0:row]
-        rs_send[:, cols] = both[row:two].astype(BF)
-        span = pl.ds(j * wide, wide)
-        rs.append(remote(rs_send.at[:, span], rs_recv.at[:, span], dev_b))
-
-    cotangent(wp, dot_send)
-    d_a = remote(dot_send, dot_rem, dev_a)
+    def other_rows(o):
+        backward(o, two, dot_rem, d_rem, False)
+
+    back = []
+
+    def send_back(o):
+        gk, gv = dk_acc[o] * SCALE, dv_acc[o]
+        if o < REACH - 1:
+            back[-1].wait_recv()
+            gk = gk + dkv_recv[o, :, 0:HD].astype(F32)
+            gv = gv + dkv_recv[o, :, HD : 2 * HD].astype(F32)
+        if o == 0:
+            gk_out[...] = gk.astype(BF)
+            gv_out[...] = gv.astype(BF)
+        else:
+            dkv_send[o - 1, :, 0:HD] = gk.astype(BF)
+            dkv_send[o - 1, :, HD : 2 * HD] = gv.astype(BF)
+            back.append(remote(dkv_send.at[o - 1], dkv_recv.at[o - 1], at(-1)))
+
+    own_rows(3)
+    own_rows(2)
     d_a.wait_recv()
     turn_d(dot_rem, d_rem, two)
-
-    back = []
-    for o in range(REACH - 1, -1, -1):
-        backward(o, two, dot_rem, d_rem, False)
-        if o > 0:
-            dkv_send[o - 1, :, 0:HD] = (dk_acc[o] * SCALE).astype(BF)
-            dkv_send[o - 1, :, HD : 2 * HD] = dv_acc[o].astype(BF)
-            back.append(remote(dkv_send.at[o - 1], dkv_recv.at[o - 1], at(-o)))
+    other_rows(3)
+    send_back(3)
+    other_rows(2)
+    own_rows(1)
+    send_back(2)
+    other_rows(1)
+    own_rows(0)
+    send_back(1)
+    other_rows(0)
 
     outs = []
 
@@ -372,23 +425,30 @@
     lo_out[...] = (lo_acc[...] + rs_recv[...].astype(F32)).astype(BF)
     put(lo_out, lo_ref)
 
-    for c in back:
-        c.wait_recv()
-    gk = dk_acc[0] * SCALE
-    gv = dv_acc[0]
-    for o in range(1, REACH):
-        gk = gk + dkv_recv[o - 1, :, 0:HD].astype(F32)
-        gv = gv + dkv_recv[o - 1, :, HD : 2 * HD].astype(F32)
-    gk_out[...] = gk.astype(BF)
-    gv_out[...] = gv.astype(BF)
+    send_back(0)
     put(gk_out, gk_ref)
     put(gv_out, gv_ref)
 
-    sent = [c for pair in kv[1:] for c in pair] + wa + [go_b, up0, down0, up1, down1]
-    sent += sibs + [far_up, far_down, o_a, d_a] + rs + back
+    sent = [c for pair in kv[1:] for c in pair] + wa + go_b + [o_a, d_a] + rs + back
+    for j in range(CHUNKS):
+        sent += [up[j], down[j], far[j]] + sibs[j]
     for c in sent:
         c.wait_send()
     for c in outs:
+        c.wait()
+
+
+def settle(*refs):
+    many = len(refs) // 3
+    came, went, held, sems = refs[:many], refs[many : 2 * many], refs[2 * many : -1], refs[-1]
+    loads = [pltpu.make_async_copy(came[i], held[i], sems.at[0, i]) for i in range(many)]
+    stores = [pltpu.make_async_copy(held[i], went[i], sems.at[1, i]) for i in range(many)]
+    for c in loads:
+        c.start()
+    for load, store in zip(loads, stores):
+        load.wait()
+        store.start()
+    for c in stores:
         c.wait()
 
 
@@ -401,7 +461,7 @@
     vm = pltpu.VMEM
     dma = pltpu.SemaphoreType.DMA
     flops = 2 * tok * width * feat * 2 + 7 * 2 * tok * tok * width * REACH
-    return pl.pallas_call(
+    found = pl.pallas_call(
         functools.partial(kernel, n, docs),
         out_shape=(
             jax.ShapeDtypeStruct((row, feat), BF),
@@ -432,6 +492,7 @@
             vm((row, feat), F32),
             vm((row, feat), BF),
             vm((width, two), F32),
+            vm((width, two), F32),
             vm((GROUP, HD, two), BF),
             vm((GROUP, HD, two), BF),
             vm((GROUP, HD, two), BF),
@@ -449,8 +510,8 @@
             vm((1, tok), jnp.int32),
             dma((4 + N_TP * GROUP,)),
             dma((7,)),
-            dma((40,)),
-            dma((40,)),
+            dma((64,)),
+            dma((64,)),
         ],
         compiler_params=pltpu.CompilerParams(
             collective_id=0, has_side_effects=True, vmem_limit_bytes=56 * 1024 * 1024
@@ -464,6 +525,13 @@
         out_weight.reshape(PARTS, width // PARTS, feat),
         grad_output,
     )
+    return pl.pallas_call(
+        settle,
+        out_shape=tuple(jax.ShapeDtypeStruct(a.shape, a.dtype) for a in found),
+        in_specs=[hbm] * 4,
+        out_specs=(hbm,) * 4,
+        scratch_shapes=[vm(a.shape, a.dtype) for a in found] + [dma((2, 4))],
+    )(*found)
 
 
 def solution(mesh):

time: 101 us -> 85.3 us (0.84)
  the two profiles are of different devices: /device:TPU:75 before, /device:TPU:1 now
where the time goes in v2:
time: 85.3 us; the launch traced here: 85 us
  Pallas kernels  84.2 us (99%)
    pallas_call x1, Pallas kernels, on_device(): pl.pallas_call(functools.partial(kernel, n, docs), out_shape=(jax.ShapeDt...  81.4 us
    pallas_call x1, Pallas kernels, on_device(): pl.pallas_call(settle, out_shape=tuple((jax.ShapeDtypeStruct(a.shape, a.d...  2.73 us

profile of v2, /device:TPU:1, one launch (start us, length us, event | category | flops | bytes accessed | tf_op | source)
XLA Modules:
  0.0 85.0 jit_solution(6757831352137788541)
XLA Ops:
  0.6 81.4 %shard_map.93 = (bf16[128,5120]{1,0:T(8,128)(2,1)}, bf16[512,640]{1,0:T(8,128)(2,1)}, bf16[512,128]{1,0:T(8,128)(2,1)}, bf16[512,128]{1,0:T(8,128)(2,1)}) custom-call(s32[32]{0:T(128)} %len_ref.1, bf16[512,640]{1,0:T(8,128)(2,1)} %q_ref.1, bf16[512,128]{1,0:T(8,128)(2,1)} %k_ref.1, bf16[512,128]{1,0:T(8,128)(2,1)} %v_ref.1, bf16[8,80,5120]{2,1,0:T(8,128)(2,1)} %bitcast.1, ...), custom_call_target="tpu_custom_call" | custom-call | flops 16106127360 | bytes 16777216 | tf_op jit(solution)/shard_map/pallas_call | solution.py:464
  82.1 2.7 %shard_map.94 = (bf16[128,5120]{1,0:T(8,128)(2,1)}, bf16[512,640]{1,0:T(8,128)(2,1)}, bf16[512,128]{1,0:T(8,128)(2,1)}, bf16[512,128]{1,0:T(8,128)(2,1)}) custom-call(bf16[128,5120]{1,0:T(8,128)(2,1)} %get-tuple-element.8.refs_0_, bf16[512,640]{1,0:T(8,128)(2,1)} %get-tuple-element.9.refs_1_, bf16[512,128]{1,0:T(8,128)(2,1)} %get-tuple-element.10.refs_2_, ...), custom_call_target="tpu_custom_call" | custom-call | tf_op jit(solution)/shard_map/pallas_call | solution.py:528
